TPU v7x, 256 devices: a whole 4x4x8 slice. The times are simulated.
256 devices in a mesh: rows: 8 (over x, core), cols: 32 (over z, y).
Axes of the slice: x: 4, y: 4, z: 8, core: 2. Of those that a mesh axis runs over, the one named last changes fastest.
Arguments:
- sinogram: float32 [8, 131072], P(None, ('rows', 'cols'))
- tiles: bfloat16 [8, 20480, 4096], P('rows', 'cols'), may hold values from -0.375 to 0.375
- tile_rows: int32 [8, 20480], P('rows', 'cols'), may hold values from 0 to 255
- tile_cols: int32 [8, 20480], P('rows', 'cols'), may hold values from 0 to 511
- tile_counts: int32 [8, 32], P('rows', 'cols'), may hold values from 1 to 640, as said below
Outputs:
- solution: float32 [8, 1048576], P(None, ('cols', 'rows'))
- residual: float32 [8, 131072], P(None, ('rows', 'cols'))
- gradient: float32 [8, 1048576], P(None, ('cols', 'rows'))
Inputs may be any that keep to these rules, and one draw needn't show every extreme that they name: tile_counts[i][j] is the number of live slots of device (i, j); slots from it on hold unused tiles; in every draw some device has all 640 slots live.
All inputs are finite; a program needn't handle non-finite values.
Results may differ from a plain program's by a relative error of at most 0.04.
Values may be sent and summed in bfloat16 or wider, within the bound.
A program may use at most 64 MiB of HBM per device.

v0:
```python
import math

import jax
import jax.numpy as jnp
from jax import lax
from jax.sharding import PartitionSpec as P

TILE = 64
RT_DEV = 256
PT_DEV = 512
ITERS = 2


epsilon = 1e-06


def tile_loop(tiles, tile_rows, tile_cols, tile_counts, table, forward):
    plates_all = tiles[0]
    row_all = tile_rows[0]
    column_all = tile_cols[0]
    count = tile_counts[0, 0]
    slots = plates_all.shape[0]
    block = math.gcd(slots, 128)
    blocks = (count + block - 1) // block
    slices = table.shape[0]
    out_tiles = RT_DEV if forward else PT_DEV

    def step(index, total):
        start = index * block
        plates = lax.dynamic_slice_in_dim(plates_all, start, block, 0).reshape(block, TILE, TILE)
        row_ids = lax.dynamic_slice_in_dim(row_all, start, block, 0)
        column_ids = lax.dynamic_slice_in_dim(column_all, start, block, 0)
        active = start + jnp.arange(block, dtype=jnp.int32) < count
        if forward:
            picked = jnp.take(table, column_ids, axis=1)
            product = jnp.einsum("stc,trc->str", picked, plates, preferred_element_type=jnp.float32)
            product = jnp.where(active[None, :, None], product, 0.0)
            return total.at[:, row_ids].add(product)
        picked = jnp.take(table, row_ids, axis=1)
        product = jnp.einsum("str,trc->stc", picked, plates, preferred_element_type=jnp.float32)
        product = jnp.where(active[None, :, None], product, 0.0)
        return total.at[:, column_ids].add(product)

    total = jnp.zeros((slices, out_tiles, TILE), jnp.float32)
    total = lax.fori_loop(0, blocks, step, total)
    return total.reshape(slices, out_tiles * TILE)


def body(sinogram, tiles, tile_rows, tile_cols, tile_counts):
    slices = sinogram.shape[0]

    def ray_group_rounded(values):
        return lax.all_gather(values.astype(jnp.bfloat16), "cols", axis=1, tiled=True)

    def pixel_totals(partial_value):
        return lax.psum_scatter(
            partial_value.astype(jnp.bfloat16), "rows", scatter_dimension=1, tiled=True
        ).astype(jnp.float32)

    def pixel_square(values):
        partial_value = jnp.sum(values * values, axis=1)
        return lax.psum(partial_value, ("rows", "cols"))

    def back_projection(residual):
        table = ray_group_rounded(residual).reshape(slices, RT_DEV, TILE)
        return pixel_totals(tile_loop(tiles, tile_rows, tile_cols, tile_counts, table, False))

    residual = sinogram
    gradient = back_projection(residual)
    direction = gradient
    gamma = pixel_square(gradient)
    solution = jnp.zeros_like(gradient)
    for step_num in range(ITERS):
        forward_table = lax.all_gather(
            direction.astype(jnp.bfloat16), "rows", axis=1, tiled=True
        ).reshape(slices, PT_DEV, TILE)
        image = lax.psum_scatter(
            tile_loop(tiles, tile_rows, tile_cols, tile_counts, forward_table, True).astype(
                jnp.bfloat16
            ),
            "cols",
            scatter_dimension=1,
            tiled=True,
        ).astype(jnp.float32)
        ray_partial_value = jnp.sum(image * image, axis=1)
        delta = lax.psum(ray_partial_value, ("rows", "cols"))
        alpha = gamma / (delta + epsilon)
        solution = solution + alpha[:, None] * direction
        residual = residual - alpha[:, None] * image
        gradient = back_projection(residual)
        if step_num + 1 < ITERS:
            fresh = pixel_square(gradient)
            direction = gradient + (fresh / (gamma + epsilon))[:, None] * direction
            gamma = fresh
    return (solution, residual, gradient)


def solution(mesh):
    return jax.shard_map(
        body,
        mesh=mesh,
        in_specs=(
            P(None, ("rows", "cols")),
            P("rows", "cols", None),
            P("rows", "cols"),
            P("rows", "cols"),
            P("rows", "cols"),
        ),
        out_specs=(P(None, ("cols", "rows")), P(None, ("rows", "cols")), P(None, ("cols", "rows"))),
        check_vma=False,
    )
```

profile of v0, /device:TPU:1, one launch (start us, length us, event | category | flops | bytes accessed | tf_op | source)
XLA Modules:
  0.0 1322.7 jit_solution(7889397496827079127)
XLA Ops:
  7.9 7.9 copy.23
  15.9 41.1 %all_gather.15 = bf16[8,16384]{1,0:T(8,128)(2,1)S(1)} all-gather(bf16[8,512]{1,0:T(8,128)(2,1)S(1)} %convert_element_type.58), channel_id=1, replica_groups=mesh['rows'=8,'cols'=32] {'cols'}, dimensions={1}, use_global_device_ids=true | all-gather | bytes 270336 | tf_op jit(solution)/shard_map/all_gather | solution.py:53
  58.8 59.6 %while.50 = (s32[]{:T(128)}, f32[8,512,64]{2,0,1:T(8,128)S(1)}, s32[]{:T(128)}, s32[640]{0:T(1024)S(1)}, s32[]{:T(128)}, /*index=5*/bf16[640,4096]{0,1:T(8,128)(...) while((s32[]{:T(128)}, f32[8,512,64]{2,0,1:T(8,128)S(1)}, ...), condition=%wide.region_2.4_spmd, body=%wide.region_0.3_spmd.sunk | while | flops 8587654 | bytes 6693047 | solution.py:45
  62.6 3.8 copy.39
  68.8 4.9 scatter_fusion
  77.5 3.8 copy.39
  83.7 4.9 scatter_fusion
  92.4 3.8 copy.39
  98.6 4.9 scatter_fusion
  107.3 3.8 copy.39
  113.5 4.9 scatter_fusion
  120.4 54.9 %reduce-scatter.6.cloned.1.call-done = bf16[8,4096]{1,0:T(8,128)(2,1)} async-done(((bf16[8,32768]{1,0:T(8,128)(2,1)}), bf16[8,4096]{1,0:T(8,128)(2,1)}) %reduce-scatter.6.cloned.1.call-update) | async-done | bytes 65552 | tf_op jit(solution)/shard_map/reduce_scatter | solution.py:56
  175.3 16.1 %all_gather.16 = bf16[8,32768]{1,0:T(8,128)(2,1)S(1)} all-gather(bf16[8,4096]{1,0:T(8,128)(2,1)} %reduce-scatter.6.cloned.1.call-done), channel_id=1, replica_groups=mesh['rows'=8,'cols'=32] {'rows'}, dimensions={1}, use_global_device_ids=true | all-gather | bytes 589824 | tf_op jit(solution)/shard_map/all_gather | solution.py:74
  193.3 57.6 %while.51 = (s32[]{:T(128)}, f32[8,256,64]{2,0,1:T(8,128)S(1)}, s32[]{:T(128)}, s32[640]{0:T(1024)S(1)}, s32[]{:T(128)}, /*index=5*/bf16[640,4096]{0,1:T(8,128)(...) while((s32[]{:T(128)}, f32[8,256,64]{2,0,1:T(8,128)S(1)}, ...), condition=%wide.region_8.11_spmd, body=%wide.region_6.10_spmd.sunk | while | flops 8587654 | bytes 6693047 | solution.py:45
  196.1 3.8 copy.40
  202.8 4.9 scatter_fusion.1
  210.5 3.8 copy.40
  214.3 2.8 fusion.66
  217.2 4.9 scatter_fusion.1
  224.9 3.8 copy.40
  228.7 2.8 fusion.66
  231.6 4.9 scatter_fusion.1
  239.3 3.8 copy.40
  243.1 2.8 fusion.66
  246.0 4.9 scatter_fusion.1
  252.5 220.7 %reduce-scatter.8.cloned.1.call-done = bf16[8,512]{1,0:T(8,128)(2,1)} async-done(((bf16[8,16384]{1,0:T(8,128)(2,1)}), bf16[8,512]{1,0:T(8,128)(2,1)}) %reduce-scatter.8.cloned.1.call-update) | async-done | bytes 8208 | tf_op jit(solution)/shard_map/reduce_scatter | solution.py:77
  474.1 80.0 %all-reduce = (f32[8]{0:T(128)S(1)}, f32[8]{0:T(128)S(1)}) all-reduce(f32[8]{0:T(128)S(1)} %fusion.31, f32[8]{0:T(128)S(1)} %fusion.34), channel_id=1, replica_groups=mesh['rows'=8,'cols'=32] {'rows','cols'}, use_global_device_ids=true, to_apply=%region_5.7 | all-reduce | flops 16 | bytes 128 | tf_op jit(solution)/shard_map/psum | solution.py:62
  554.8 36.0 %all_gather.17 = bf16[8,16384]{1,0:T(8,128)(2,1)S(1)} all-gather(bf16[8,512]{1,0:T(8,128)(2,1)S(1)} %fusion.38), channel_id=1, replica_groups=mesh['rows'=8,'cols'=32] {'cols'}, dimensions={1}, use_global_device_ids=true | all-gather | bytes 270336 | tf_op jit(solution)/shard_map/all_gather | solution.py:53
  592.6 59.6 %while.52 = (s32[]{:T(128)}, f32[8,512,64]{2,0,1:T(8,128)S(1)}, s32[]{:T(128)}, s32[640]{0:T(1024)S(1)}, s32[]{:T(128)}, /*index=5*/bf16[640,4096]{0,1:T(8,128)(...) while((s32[]{:T(128)}, f32[8,512,64]{2,0,1:T(8,128)S(1)}, ...), condition=%wide.region_14.17_spmd, body=%wide.region_12.16_spmd.sunk | while | flops 8587654 | bytes 6693047 | solution.py:45
  596.4 3.8 copy.41
  602.6 4.9 scatter_fusion.2
  611.3 3.8 copy.41
  617.5 4.9 scatter_fusion.2
  626.2 3.8 copy.41
  632.4 4.9 scatter_fusion.2
  641.1 3.8 copy.41
  647.3 4.9 scatter_fusion.2
  654.2 52.9 %reduce-scatter.10.cloned.1.call-done = bf16[8,4096]{1,0:T(8,128)(2,1)} async-done(((bf16[8,32768]{1,0:T(8,128)(2,1)}), bf16[8,4096]{1,0:T(8,128)(2,1)}) %reduce-scatter.10.cloned.1.call-update) | async-done | bytes 65552 | tf_op jit(solution)/shard_map/reduce_scatter | solution.py:56
  708.1 78.4 %psum.30 = f32[8]{0:T(128)S(1)} all-reduce(f32[8]{0:T(128)S(1)} %fusion.30), channel_id=1, replica_groups=mesh['rows'=8,'cols'=32] {'rows','cols'}, use_global_device_ids=true, to_apply=%region_17.20 | all-reduce | flops 8 | bytes 64 | tf_op jit(solution)/shard_map/psum | solution.py:62
  787.5 13.8 %all_gather.18 = bf16[8,32768]{1,0:T(8,128)(2,1)S(1)} all-gather(bf16[8,4096]{1,0:T(8,128)(2,1)S(1)} %fusion.33), channel_id=1, replica_groups=mesh['rows'=8,'cols'=32] {'rows'}, dimensions={1}, use_global_device_ids=true | all-gather | bytes 589824 | tf_op jit(solution)/shard_map/all_gather | solution.py:74
  803.2 57.8 %while.53 = (s32[]{:T(128)}, f32[8,256,64]{2,0,1:T(8,128)S(1)}, s32[]{:T(128)}, s32[640]{0:T(1024)S(1)}, s32[]{:T(128)}, /*index=5*/bf16[640,4096]{0,1:T(8,128)(...) while((s32[]{:T(128)}, f32[8,256,64]{2,0,1:T(8,128)S(1)}, ...), condition=%wide.region_20.23_spmd, body=%wide.region_18.22_spmd.sunk | while | flops 8587654 | bytes 6693047 | solution.py:45
  806.0 3.8 copy.42
  809.8 2.8 fusion.72
  812.7 4.9 scatter_fusion.3
  820.4 3.8 copy.42
  824.2 2.8 fusion.72
  827.1 4.9 scatter_fusion.3
  834.8 3.8 copy.42
  841.5 4.9 scatter_fusion.3
  849.2 3.8 copy.42
  855.9 4.9 scatter_fusion.3
  862.5 217.9 %reduce-scatter.12.cloned.1.call-done = bf16[8,512]{1,0:T(8,128)(2,1)} async-done(((bf16[8,16384]{1,0:T(8,128)(2,1)}), bf16[8,512]{1,0:T(8,128)(2,1)}) %reduce-scatter.12.cloned.1.call-update) | async-done | bytes 8208 | tf_op jit(solution)/shard_map/reduce_scatter | solution.py:77
  1081.2 79.8 %psum.31 = f32[8]{0:T(128)S(1)} all-reduce(f32[8]{0:T(128)S(1)} %fusion.36), channel_id=1, replica_groups=mesh['rows'=8,'cols'=32] {'rows','cols'}, use_global_device_ids=true, to_apply=%region_23.26 | all-reduce | flops 8 | bytes 64 | tf_op jit(solution)/shard_map/psum | solution.py:86
  1162.4 35.9 %all_gather.19 = bf16[8,16384]{1,0:T(8,128)(2,1)S(1)} all-gather(bf16[8,512]{1,0:T(8,128)(2,1)S(1)} %get-tuple-element.357), channel_id=1, replica_groups=mesh['rows'=8,'cols'=32] {'cols'}, dimensions={1}, use_global_device_ids=true | all-gather | bytes 270336 | tf_op jit(solution)/shard_map/all_gather | solution.py:53
  1200.1 59.6 %while.54 = (s32[]{:T(128)}, f32[8,512,64]{2,0,1:T(8,128)S(1)}, s32[]{:T(128)}, s32[640]{0:T(1024)S(1)}, s32[]{:T(128)}, /*index=5*/bf16[640,4096]{0,1:T(8,128)(...) while((s32[]{:T(128)}, f32[8,512,64]{2,0,1:T(8,128)S(1)}, ...), condition=%wide.region_26.29_spmd, body=%wide.region_24.28_spmd.sunk | while | flops 8587654 | bytes 6693047 | solution.py:45
  1203.9 3.8 copy.43
  1210.1 4.9 scatter_fusion.4
  1218.8 3.8 copy.43
  1225.0 4.9 scatter_fusion.4
  1233.7 3.8 copy.43
  1239.9 4.9 scatter_fusion.4
  1248.6 3.8 copy.43
  1254.8 4.9 scatter_fusion.4
  1262.4 52.2 %reduce-scatter.14.cloned.1.call-done = bf16[8,4096]{1,0:T(8,128)(2,1)} async-done(((bf16[8,32768]{1,0:T(8,128)(2,1)}), bf16[8,4096]{1,0:T(8,128)(2,1)}) %reduce-scatter.14.cloned.1.call-update) | async-done | bytes 65552 | tf_op jit(solution)/shard_map/reduce_scatter | solution.py:56
  (182 shorter events, 130.2 us)
Async XLA Ops:
  7.2 168.1 %reduce-scatter.6.cloned.1.call-start = ((), (), s32[]{:S(2)}) async-start(), calls=%async_computation.5 | async-start | bytes 589824 | tf_op jit(solution)/shard_map/reduce_scatter | solution.py:56
  7.9 7.9 copy-start.4
  7.9 7.9 copy-start.5
  7.9 8.0 copy-start.2
  120.3 352.9 %reduce-scatter.8.cloned.1.call-start = ((), (), s32[]{:S(2)}) async-start(), calls=%async_computation.6 | async-start | bytes 270336 | tf_op jit(solution)/shard_map/reduce_scatter | solution.py:77
  250.9 1.4 copy-start
  252.3 454.8 %reduce-scatter.10.cloned.1.call-start = ((), (), s32[]{:S(2)}) async-start(), calls=%async_computation.7 | async-start | bytes 589824 | tf_op jit(solution)/shard_map/reduce_scatter | solution.py:56
  654.1 426.2 %reduce-scatter.12.cloned.1.call-start = ((), (), s32[]{:S(2)}) async-start(), calls=%async_computation.8 | async-start | bytes 270336 | tf_op jit(solution)/shard_map/reduce_scatter | solution.py:77
  861.1 299.9 %copy-start.3 = (bf16[8,512]{1,0:T(8,128)(2,1)S(1)}, bf16[8,512]{1,0:T(8,128)(2,1)}, u32[]{:S(2)}) copy-start(bf16[8,512]{1,0:T(8,128)(2,1)} %reduce-scatter.8.cloned.1.call-done) | copy-start | bytes 24580
  862.4 452.2 %reduce-scatter.14.cloned.1.call-start = ((), (), s32[]{:S(2)}) async-start(), calls=%async_computation.9 | async-start | bytes 589824 | tf_op jit(solution)/shard_map/reduce_scatter | solution.py:56
  1259.9 1.8 copy-start.1
Sparse Core Ops, SparseCore 0:
  120.4 54.7 reduce-scatter.5
  252.4 220.7 reduce-scatter.7
  654.2 52.8 reduce-scatter.9
  862.5 217.7 reduce-scatter.11
  1261.8 52.8 reduce-scatter.13
where the time goes:
time: 1330 us; the launch traced here: 1320 us
  waiting for transfers between devices  599 us (45%)
  blocking collectives  381 us (29%)
  local copies, waits for them, and re-layouts  153 us (12%)
  other arithmetic  123 us (9%)
  matrix products  50.2 us (4%)
  between operations  14.7 us (1%)
    reduce_scatter x2, waiting for transfers between devices, body(): lax.psum_scatter(tile_loop(tiles, tile_rows, tile_cols, tile_counts, forw...  439 us
    reduce_scatter x3, waiting for transfers between devices, pixel_totals(): lax.psum_scatter(partial_value.astype(jnp.bfloat16), 'rows', scatter_dime...  160 us
    psum x2, blocking collectives, pixel_square(): return lax.psum(partial_value, ('rows', 'cols'))  158 us
    all_gather x3, blocking collectives, ray_group_rounded(): lax.all_gather(values.astype(jnp.bfloat16), 'cols', axis=1, tiled=True)  113 us
    psum x1, blocking collectives, body(): delta = lax.psum(ray_partial_value, ('rows', 'cols'))  79.8 us
    reshape x20, local copies, waits for them, and re-layouts, step(): lax.dynamic_slice_in_dim(plates_all, start, block, 0)  76.3 us
    scatter-add x12, other arithmetic, step(): return total.at[:, column_ids].add(product)  59 us
    scatter-add x8, other arithmetic, step(): return total.at[:, row_ids].add(product)  39.4 us
  transfers between devices with their start and end apart: 5, of which 5 were waited for; matrix products, arithmetic and copies ran while one was open for 0% of the time, Pallas kernels for 0%

commit v1 on v0

v1 whole, which is shorter than its diff:
```python
import functools

import jax
import jax.numpy as jnp
from jax import lax
from jax.experimental import pallas as pl
from jax.experimental.pallas import tpu as pltpu
from jax.sharding import PartitionSpec as P

BF, F32 = jnp.bfloat16, jnp.float32
SL = 640
EPS = 1e-6
MESH = pl.DeviceIdType.MESH

def lane(shape):
    return lax.broadcasted_iota(jnp.int32, shape, len(shape) - 1)

def build_w(t_hbm, tv, st, w, sems, chunk=128):
    n = SL // chunk
    def cp(k):
        return pltpu.make_async_copy(t_hbm.at[pl.ds(k * chunk, chunk)], tv.at[k % 2], sems.at[k % 2])
    cp(0).start()
    for k in range(n):
        if k + 1 < n:
            cp(k + 1).start()
        cp(k).wait()
        for q in range(32):
            st[pl.ds(q, chunk, stride=32), :] = tv[k % 2, :, q * 128:(q + 1) * 128].astype(F32)
        @pl.loop(0, chunk // 4)
        def _(b):
            w[k * (chunk // 4) + b] = st[pl.ds(pl.multiple_of(b * 128, 128), 128), :].astype(BF)

def build_oh(rows_v, cols_v, live, ohr, ohc):
    r = rows_v[...]; c = cols_v[...]
    ok = lane((1, SL)) < live
    r = jnp.where(ok, r, -1); c = jnp.where(ok, c, -1)
    @pl.loop(0, 256 // 32)
    def _(i):
        s = lax.broadcasted_iota(jnp.int32, (32, SL), 0) + i * 32
        ohr[pl.ds(pl.multiple_of(i * 32, 32), 32), :] = jnp.where(s == r, 1.0, 0.0).astype(BF)
    @pl.loop(0, 512 // 32)
    def _(i):
        s = lax.broadcasted_iota(jnp.int32, (32, SL), 0) + i * 32
        ohc[pl.ds(pl.multiple_of(i * 32, 32), 32), :] = jnp.where(s == c, 1.0, 0.0).astype(BF)

def rep_mat():
    i = lax.broadcasted_iota(jnp.int32, (128, 512), 0)
    j = lax.broadcasted_iota(jnp.int32, (128, 512), 1)
    return jnp.where(i == (j // 128) * 32 + j % 32, 1.0, 0.0).astype(BF)

def table_b(x, tab):
    e = rep_mat()
    flat = tab.reshape(256 * 16, 128)
    for quad in range(2):
        xs = x[:, :, quad * 128:(quad + 1) * 128].reshape(512, 128)
        y = jnp.dot(xs, e, preferred_element_type=F32)
        for b in range(4):
            s = quad * 4 + b
            yb = y[:, b * 128:(b + 1) * 128].reshape(32, 16, 128)
            for par in range(2):
                flat[pl.ds(par * 8 + s, 256, stride=16), :] = yb[:, par * 8:par * 8 + 8].reshape(256, 128)

def table_a(d, tab):
    low = lane((1, 128)) < 64
    flat = tab.reshape(512 * 16, 128)
    for sp in range(4):
        x = d[:, :, sp * 128:(sp + 1) * 128].reshape(512, 128).astype(F32)
        xr = pltpu.roll(x, 64, 1)
        for s, par, v in ((2 * sp, 0, x), (2 * sp, 1, xr), (2 * sp + 1, 0, xr), (2 * sp + 1, 1, x)):
            v = jnp.where(low, v, 0.0) if par == 0 else jnp.where(low, 0.0, v)
            flat[pl.ds(par * 8 + s, 512, stride=16), :] = v

def main_b(idx, tab, w, p, unroll=20):
    low = lane((8, 128)) < 64
    grp = lane((16, 128)) // 32
    @pl.loop(0, SL // 4 // unroll)
    def _(o):
        lhs, out = [], []
        for u in range(unroll):
            ls = []
            for k in range(4):
                t = idx[0, (o * unroll + u) * 4 + k]
                v = tab[t]
                ls.append(jnp.where(grp == k, v, 0.0).astype(BF))
            lhs.append(jnp.concatenate(ls, 0))
        for u in range(unroll):
            out.append(jnp.dot(lhs[u], w[o * unroll + u], preferred_element_type=F32))
        for u in range(unroll):
            for k in range(4):
                v = jnp.where(low, out[u][16 * k:16 * k + 8], out[u][16 * k + 8:16 * k + 16])
                v = v + pltpu.roll(v, 64, 1)
                p[pl.ds(pl.multiple_of(((o * unroll + u) * 4 + k) * 8, 8), 8), :] = v

def main_a(idx, tab, w, p, unroll=20):
    grp = lane((16, 128)) // 32
    @pl.loop(0, SL // 4 // unroll)
    def _(o):
        lhs, out = [], []
        for u in range(unroll):
            ls = []
            for k in range(4):
                t = idx[0, (o * unroll + u) * 4 + k]
                ls.append(tab[t].astype(BF))
            lhs.append(jnp.concatenate(ls, 0))
        for u in range(unroll):
            out.append(lax.dot_general(lhs[u], w[o * unroll + u], (((1,), (1,)), ((), ())), preferred_element_type=F32))
        for u in range(unroll):
            for k in range(4):
                p[pl.ds(pl.multiple_of(((o * unroll + u) * 4 + k) * 16, 16), 16), :] = jnp.where(grp == k, out[u][16 * k:16 * k + 16], 0.0)

def hilo(m, two):
    hi = m.astype(BF)
    if not two:
        return (hi,)
    return hi, (m - hi.astype(F32)).astype(BF)

def scatter_b(p, ohc, out, two=False):
    low = lane((1, 128)) < 64
    for sp in range(4):
        m = jnp.where(low, p[pl.ds(2 * sp, SL, stride=8), :], p[pl.ds(2 * sp + 1, SL, stride=8), :])
        y = sum(jnp.dot(ohc[...], h, preferred_element_type=F32) for h in hilo(m, two))
        out[:, :, sp * 128:(sp + 1) * 128] = y.astype(BF).reshape(8, 64, 128)

def scatter_a(p, ohr, out, two=False):
    grp = lane((1, 128)) // 32
    for quad in range(2):
        halves = []
        for par in range(2):
            tot = None
            for b in range(4):
                m = p[pl.ds(par * 8 + quad * 4 + b, SL, stride=16), :]
                y = sum(jnp.dot(ohr[...], h, preferred_element_type=F32) for h in hilo(m, two))
                y = y + pltpu.roll(y, 32, 1)
                y = y + pltpu.roll(y, 64, 1)
                tot = y if b == 0 else jnp.where(grp == b, y, tot)
            halves.append(tot.reshape(32, 8, 128))
        out[:, :, quad * 128:(quad + 1) * 128] = jnp.concatenate(halves, 1).astype(BF)


def wait_bytes(buf, n, sem):
    pltpu.make_async_copy(buf.at[pl.ds(0, n)], buf.at[pl.ds(0, n)], sem).wait()


def gather_start(axis, n, buf, send, recv):
    me = lax.axis_index(axis)

    @pl.loop(1, n)
    def _(d):
        to = lax.rem(me + d, n)
        pltpu.make_async_remote_copy(buf.at[me], buf.at[me], send, recv, device_id={axis: to}, device_id_type=MESH).start()


def spread_start(axis, n, parts, buf, send, recv):
    me = lax.axis_index(axis)

    @pl.loop(1, n)
    def _(d):
        to = lax.rem(me + d, n)
        pltpu.make_async_remote_copy(parts.at[to], buf.at[me], send, recv, device_id={axis: to}, device_id_type=MESH).start()

    buf[me] = parts[me]


def group_sums(x, width):
    i = lax.broadcasted_iota(jnp.int32, (256, 8 * width), 0) // 32
    j = lax.broadcasted_iota(jnp.int32, (256, 8 * width), 1) // width
    return jnp.dot(x, jnp.where(i == j, 1.0, 0.0), precision=lax.Precision.HIGHEST, preferred_element_type=F32)


def kernel(nr, nc, rows_s, cols_s, rows_v, cols_v, count, t_hbm, sino, sol_o, res_o, grad_o,
           tv, st, w, ohr, ohc, tb, ta, pb, pa,
           r_all, q0_all, q1_all, rf, g0_all, g1_all, pp0, pp1, pp2, gp0, gp1, gp2, rp0, rp1, qp0, qp1, sc0, sc1,
           g_sh, r_sh, q_sh, sems, tsem):
    i, j = lax.axis_index("rows"), lax.axis_index("cols")
    barrier = pltpu.get_barrier_semaphore()

    @pl.loop(1, nc)
    def _(d):
        pl.semaphore_signal(barrier, inc=1, device_id={"cols": lax.rem(j + d, nc)}, device_id_type=MESH)

    @pl.loop(1, nr)
    def _(d):
        pl.semaphore_signal(barrier, inc=1, device_id={"rows": lax.rem(i + d, nr)}, device_id_type=MESH)

    r_sh[...] = sino[...]
    r_all[j] = sino[...].astype(BF)
    build_oh(rows_v, cols_v, count[0, 0], ohr, ohc)
    pl.semaphore_wait(barrier, nc + nr - 2)
    gather_start("cols", nc, r_all, sems.at[0, 0], sems.at[1, 0])
    build_w(t_hbm, tv, st, w, tsem)
    wait_bytes(r_all, nc - 1, sems.at[1, 0])

    def back(x, parts, buf, ph):
        table_b(x, tb)
        main_b(rows_s, tb, w, pb)
        scatter_b(pb, ohc, parts)
        spread_start("rows", nr, parts, buf, sems.at[0, ph], sems.at[1, ph])
        wait_bytes(buf, nr - 1, sems.at[1, ph])
        return jnp.sum(buf[...].astype(F32), 0)

    def forward(d_all, parts, buf, ph):
        wait_bytes(d_all, nr - 1, sems.at[1, ph])
        table_a(d_all, ta)
        main_a(cols_s, ta, w, pa)
        scatter_a(pa, ohr, parts)
        spread_start("cols", nc, parts, buf, sems.at[0, ph + 1], sems.at[1, ph + 1])
        wait_bytes(buf, nc - 1, sems.at[1, ph + 1])
        return jnp.sum(buf[...].astype(F32), 0)

    def row_sum(v):
        return jnp.sum(v.reshape(-1, 256), 0, keepdims=True)

    def exchange(vals, buf, ph):
        buf[i] = jnp.concatenate(vals + [jnp.zeros((8 - len(vals), 256), F32)], 0)
        gather_start("rows", nr, buf, sems.at[0, ph], sems.at[1, ph])
        wait_bytes(buf, nr - 1, sems.at[1, ph])
        tot = jnp.sum(buf[...], 0)
        return group_sums(tot, 32), group_sums(tot, 64)

    g = back(r_all, pp0, gp0, 1)
    g_sh[...] = g
    g0_all[i] = g.astype(BF)
    gather_start("rows", nr, g0_all, sems.at[0, 2], sems.at[1, 2])
    q = forward(g0_all, rp0, qp0, 2)
    q_sh[...] = q
    q0_all[j] = q.astype(BF)
    gather_start("cols", nc, q0_all, sems.at[0, 4], sems.at[1, 4])
    wait_bytes(q0_all, nc - 1, sems.at[1, 4])
    r0f, q0f = r_all[...].astype(F32), q0_all[...].astype(F32)
    n32, n64 = exchange([row_sum(r0f * q0f), row_sum(q0f * q0f)], sc0, 5)
    alpha = n32[0:1] / (n32[1:2] + EPS)
    alpha_p = n64[0:1] / (n64[1:2] + EPS)
    r1f = r_all[...].astype(F32) - alpha * q0_all[...].astype(F32)
    rf[...] = r1f
    wait_bytes(r_all, nc - 1, sems.at[0, 0])
    r_all[...] = r1f.astype(BF)
    r_sh[...] = r_sh[...] - alpha * q_sh[...]
    sol_o[...] = alpha_p * g_sh[...]
    g1 = back(r_all, pp1, gp1, 6)
    g1_all[i] = g1.astype(BF)
    gather_start("rows", nr, g1_all, sems.at[0, 7], sems.at[1, 7])
    qh = forward(g1_all, rp1, qp1, 7)
    q1_all[j] = qh.astype(BF)
    gather_start("cols", nc, q1_all, sems.at[0, 9], sems.at[1, 9])
    wait_bytes(q1_all, nc - 1, sems.at[1, 9])
    q1f, q0f = q1_all[...].astype(F32), q0_all[...].astype(F32)
    m32, m64 = exchange([row_sum(rf[...] * q1f), row_sum(q1f * q1f), row_sum(q1f * q0f)], sc1, 10)

    def second(n, m):
        beta = m[0:1] / (n[0:1] + EPS)
        delta = m[1:2] + 2.0 * beta * m[2:3] + beta * beta * n[1:2]
        return beta, m[0:1] / (delta + EPS)

    beta, alpha = second(n32, m32)
    beta_p, alpha_p = second(n64, m64)
    r2f = rf[...] - alpha * (q1_all[...].astype(F32) + beta * q0_all[...].astype(F32))
    r_all[...] = r2f.astype(BF)
    res_o[...] = r_sh[...] - alpha * (qh + beta * q_sh[...])
    sol_o[...] = sol_o[...] + alpha_p * (g1 + beta_p * g_sh[...])
    grad_o[...] = back(r_all, pp2, gp2, 11)
    for ph, buf, n in ((1, gp0, nr), (2, g0_all, nr), (3, qp0, nc), (4, q0_all, nc), (5, sc0, nr), (6, gp1, nr),
                       (7, g1_all, nr), (8, qp1, nc), (9, q1_all, nc), (10, sc1, nr), (11, gp2, nr)):
        wait_bytes(buf, n - 1, sems.at[0, ph])


def solution(mesh):
    nr, nc = mesh.shape["rows"], mesh.shape["cols"]

    def body(sinogram, tiles, tile_rows, tile_cols, tile_counts):
        sino = sinogram.reshape(8, 8, 32, 2).transpose(3, 1, 0, 2).reshape(16, 256)
        vm, sm = pl.BlockSpec(memory_space=pltpu.VMEM), pl.BlockSpec(memory_space=pltpu.SMEM)
        ray, pix = (nc, 16, 256), (nr, 64, 512)
        sol, res, grad = pl.pallas_call(
            functools.partial(kernel, nr, nc),
            out_shape=(jax.ShapeDtypeStruct((64, 512), F32), jax.ShapeDtypeStruct((16, 256), F32), jax.ShapeDtypeStruct((64, 512), F32)),
            in_specs=[sm, sm, vm, vm, sm, pl.BlockSpec(memory_space=pl.ANY), vm],
            out_specs=(vm, vm, vm),
            scratch_shapes=[
                pltpu.VMEM((2, 128, 4096), BF), pltpu.VMEM((128 * 32, 128), F32), pltpu.VMEM((160, 128, 128), BF),
                pltpu.VMEM((256, SL), BF), pltpu.VMEM((512, SL), BF), pltpu.VMEM((256, 16, 128), F32), pltpu.VMEM((512, 16, 128), F32),
                pltpu.VMEM((SL * 8, 128), F32), pltpu.VMEM((SL * 16, 128), F32),
                pltpu.VMEM(ray, BF), pltpu.VMEM(ray, BF), pltpu.VMEM(ray, BF), pltpu.VMEM(ray, F32),
                pltpu.VMEM(pix, BF), pltpu.VMEM(pix, BF),
                pltpu.VMEM(pix, BF), pltpu.VMEM(pix, BF), pltpu.VMEM(pix, BF), pltpu.VMEM(pix, BF), pltpu.VMEM(pix, BF), pltpu.VMEM(pix, BF),
                pltpu.VMEM(ray, BF), pltpu.VMEM(ray, BF), pltpu.VMEM(ray, BF), pltpu.VMEM(ray, BF),
                pltpu.VMEM((nr, 8, 256), F32), pltpu.VMEM((nr, 8, 256), F32),
                pltpu.VMEM((64, 512), F32), pltpu.VMEM((16, 256), F32), pltpu.VMEM((16, 256), F32),
                pltpu.SemaphoreType.DMA((2, 12)), pltpu.SemaphoreType.DMA((2,)),
            ],
            compiler_params=pltpu.CompilerParams(collective_id=0, has_side_effects=True, vmem_limit_bytes=60 * 2**20),
            name="cgls",
        )(tile_rows, tile_cols, tile_rows, tile_cols, tile_counts, tiles.reshape(SL, 4096), sino)

        def pixels(x):
            return x.reshape(64, 8, 64).transpose(1, 0, 2).reshape(8, 4096)

        rays = res.reshape(2, 8, 8, 32).transpose(2, 1, 3, 0).reshape(8, 512)
        return pixels(sol), rays, pixels(grad)

    return jax.shard_map(
        body,
        mesh=mesh,
        in_specs=(
            P(None, ("rows", "cols")),
            P("rows", "cols", None),
            P("rows", "cols"),
            P("rows", "cols"),
            P("rows", "cols"),
        ),
        out_specs=(P(None, ("cols", "rows")), P(None, ("rows", "cols")), P(None, ("cols", "rows"))),
        check_vma=False,
    )
```

time: 1330 us -> 154 us (0.12)
  waiting for transfers between devices: 599 us -> 0 us
  blocking collectives: 381 us -> 0 us
  local copies, waits for them, and re-layouts: 153 us -> 6.99 us
  Pallas kernels: 0 us -> 146 us
  other arithmetic: 123 us -> 0 us
  matrix products: 50.2 us -> 0 us
  between operations: 14.7 us -> 1.32 us
    reduce_scatter x5 -> x0, waiting for transfers between devices: 599 us -> none  [the longest x2 439 us: body(): lax.psum_scatter(tile_loop(tiles, tile_rows, tile_cols, tile_counts, forw...]
    psum x3 -> x0, blocking collectives: 238 us -> none  [the longest x2 158 us: pixel_square(): return lax.psum(partial_value, ('rows', 'cols'))]
    pallas_call x0 -> x1, Pallas kernels: none -> 146 us  [body(): pl.pallas_call(functools.partial(kernel, nr, nc), out_shape=(jax.ShapeDty...]
    all_gather x5 -> x0, blocking collectives: 143 us -> none  [the longest x3 113 us: ray_group_rounded(): lax.all_gather(values.astype(jnp.bfloat16), 'cols', axis=1, tiled=True)]
    scatter-add x20 -> x0, other arithmetic: 98.4 us -> none  [the longest x12 59 us: step(): return total.at[:, column_ids].add(product)]
    reshape x25 -> x7, local copies, waits for them, and re-layouts: 80.1 us -> 5.21 us  [the longest x4 3.55 us: pixels(): return x.reshape(64, 8, 64).transpose(1, 0, 2).reshape(8, 4096)]
    dot_general x20 -> x0, matrix products: 50.2 us -> none  [the longest x12 27.6 us: step(): jnp.einsum('str,trc->stc', picked, plates, preferred_element_type=jnp.flo...]
    gather x20 -> x0, local copies, waits for them, and re-layouts: 26.1 us -> none  [the longest x12 20.6 us: step(): picked = jnp.take(table, row_ids, axis=1)]
  transfers between devices with their start and end apart: 5 -> 0, of which waited for: 5 -> 0; matrix products, arithmetic and copies ran while one was open for 0% -> 0% of each run, Pallas kernels for 0% -> 0%
where the time goes in v1:
time: 154 us
  Pallas kernels  146 us (95%)
  local copies, waits for them, and re-layouts  6.99 us (5%)
    pallas_call x1, Pallas kernels, body(): pl.pallas_call(functools.partial(kernel, nr, nc), out_shape=(jax.ShapeDty...  146 us
    reshape x4, local copies, waits for them, and re-layouts, pixels(): return x.reshape(64, 8, 64).transpose(1, 0, 2).reshape(8, 4096)  3.55 us

profile of v1, /device:TPU:1, one launch (start us, length us, event | category | flops | bytes accessed | tf_op | source)
XLA Modules:
  0.0 153.9 jit_solution(4706735056738797398)
XLA Ops:
  0.6 0.8 copy.12
  1.5 0.1 copy.13
  1.6 0.7 reshape.35.sino
  3.0 145.6 %cgls.1 = (f32[64,512]{1,0:T(8,128)}, f32[16,256]{1,0:T(8,128)}, f32[64,512]{1,0:T(8,128)}) custom-call(s32[1,640]{1,0:T(1,128)} %rows_v.1, s32[1,640]{1,0:T(1,128)} %cols_v.1, s32[1,640]{1,0:T(1,128)} %rows_v.1, s32[1,640]{1,0:T(1,128)} %cols_v.1, s32[1,1]{1,0:T(1,128)S(6)} %copy.18.count, bf16[640,4096]{1,0:T(8,128)(2,1)} %bitcast.11, f32[16,256]{1,0:T(8,128)} %reshape.35.sino), custom_call_target="tpu_custom_call" | custom-call | tf_op jit(solution)/shard_map/cgls/pallas_call | solution.py:273
  148.6 1.0 reshape.36
  149.6 0.1 copy.14
  149.7 0.8 reshape.37
  150.4 1.0 reshape.40
  151.4 0.1 copy.16
  151.5 0.8 reshape.41
  152.3 0.8 reshape.38
  153.1 0.2 copy.15
  153.2 0.7 copy.17

commit v2 on v0

v2 whole, which is shorter than its diff:
```python
import functools

import jax
import jax.numpy as jnp
from jax import lax
from jax.experimental import pallas as pl
from jax.experimental.pallas import tpu as pltpu
from jax.sharding import PartitionSpec as P

BF, F32 = jnp.bfloat16, jnp.float32
SL = 640
EPS = 1e-6
MESH = pl.DeviceIdType.MESH
CHUNK = 64
PAD = 40


def lane(shape):
    return lax.broadcasted_iota(jnp.int32, shape, len(shape) - 1)


def sub(shape):
    return lax.broadcasted_iota(jnp.int32, shape, len(shape) - 2)


def tile_copy(t_hbm, tv, sems, k):
    return pltpu.make_async_copy(t_hbm.at[pl.ds(k * CHUNK, CHUNK)], tv.at[k], sems.at[k])


def build_w(tv, st, w, k):
    s = st.at[k % 2]
    for q in range(32):
        s[pl.ds(q, CHUNK, stride=PAD), :] = tv[k, :, q * 128:(q + 1) * 128].astype(F32)
    for b in range(CHUNK // 4):
        w[k * (CHUNK // 4) + b] = jnp.concatenate([s[(b * 4 + m) * PAD:(b * 4 + m) * PAD + 32, :] for m in range(4)], 0).astype(BF)


def build_wt(w, wt, first, end):
    eye = jnp.where(lane((128, 128)) == sub((128, 128)), 1.0, 0.0).astype(BF)

    @pl.loop(first // 20, end // 20)
    def _(o):
        for u in range(20):
            wt[o * 20 + u] = lax.dot_general(eye, w[o * 20 + u], (((1,), (1,)), ((), ())), preferred_element_type=F32).astype(BF)


def build_oh(rows_v, cols_v, live, ohr, ohc):
    at = lane((1, SL))
    perm = jnp.where(sub((SL, SL)) == (at % (SL // 4)) * 4 + at // (SL // 4), 1.0, 0.0).astype(BF)
    ids = jnp.where(at < live, rows_v[...], -1).astype(F32)
    r = jnp.dot(jnp.broadcast_to(ids, (8, SL)).astype(BF), perm, preferred_element_type=F32)[0:1].astype(jnp.int32)
    c = jnp.where(at < live, cols_v[...], -1)

    def fill(oh, n, ids):
        @pl.loop(0, n // 32)
        def _(i):
            s = sub((32, SL)) + i * 32
            oh[pl.ds(pl.multiple_of(i * 32, 32), 32), :] = jnp.where(s == ids, 1.0, 0.0).astype(BF)

    fill(ohr, 256, r)
    fill(ohc, 512, c)


def table_b(x, tab):
    flat = tab.reshape(256 * 8, 128)
    i, j = sub((128, 512)), lane((128, 512))
    e = jnp.where(i == (j // 128) * 32 + j % 32, 1.0, 0.0).astype(BF)
    y = jnp.dot(x[...].reshape(512, 128), e, preferred_element_type=F32)
    for s in range(4):
        ys = y[:, s * 128:(s + 1) * 128].reshape(32, 16, 128)
        for par in range(2):
            flat[pl.ds(par * 4 + s, 256, stride=8), :] = ys[:, par * 8:par * 8 + 8].reshape(256, 128)


def table_a(d, tab):
    flat = tab.reshape(512 * 8, 128)
    for sp in range(2):
        x = d[:, :, sp * 128:(sp + 1) * 128].reshape(512, 128).astype(F32)
        xr = pltpu.roll(x, 64, 1)
        for s, par, v in ((2 * sp, 0, x), (2 * sp, 1, xr), (2 * sp + 1, 0, xr), (2 * sp + 1, 1, x)):
            flat[pl.ds(par * 4 + s, 512, stride=8), :] = v


def main(idx, tab, w, p, forward, unroll):
    grp = lane((8, 128)) // 32
    half = (lane((8, 128)) // 64) == (sub((8, 128)) // 4)

    pad = PAD if forward else 32

    @pl.loop(0, SL // 4 // unroll)
    def _(o):
        lhs, out = [], []
        for u in range(unroll):
            ls = []
            for k in range(4):
                t = idx[0, (o * unroll + u) * 4 + k]
                ls.append(jnp.where(half if forward else grp == k, tab[t], 0.0))
            lhs.append(jnp.concatenate(ls, 0).astype(BF))
        for u in range(unroll):
            out.append(jnp.dot(lhs[u], w[o * unroll + u], preferred_element_type=F32))
        for u in range(unroll):
            p[pl.ds(pl.multiple_of((o * unroll + u) * pad, 8), 32), :] = out[u]


def scatter_b(p, ohc, out):
    low = lane((1, 128)) < 64
    for sp in range(2):
        fs = []
        for s in (2 * sp, 2 * sp + 1):
            m = jnp.where(low, p[pl.ds(s, SL, stride=8), :], p[pl.ds(4 + s, SL, stride=8), :])
            fs.append(m + pltpu.roll(m, 64, 1))
        x = jnp.where(low, fs[0], fs[1]).astype(BF)
        y = jnp.dot(ohc[...], x, preferred_element_type=F32)
        out[:, :, sp * 128:(sp + 1) * 128] = y.astype(BF).reshape(8, 64, 128)


def scatter_a(p, ohr, out):
    grp = lane((1, 128)) // 32
    halves = []
    for par in range(2):
        xs = []
        for k in range(4):
            x = None
            for s in range(4):
                m = p[pl.ds(k * 8 + par * 4 + s, SL // 4, stride=PAD), :]
                if s != k:
                    m = pltpu.roll(m, (32 * (s - k)) % 128, 1)
                x = m if s == 0 else jnp.where(grp == s, m, x)
            xs.append(x.astype(BF))
        y = jnp.dot(ohr[...], jnp.concatenate(xs, 0), preferred_element_type=F32)
        halves.append(y.reshape(32, 8, 128))
    out[...] = jnp.concatenate(halves, 1).astype(BF)


def wait_bytes(buf, n, sem):
    pltpu.make_async_copy(buf.at[pl.ds(0, n)], buf.at[pl.ds(0, n)], sem).wait()


def far_first(a, n):
    return n // 2 + ((a + 1) // 2) * (1 - 2 * (a % 2))


def col_peer(j, m, ny, nz):
    z, y = j // ny, j % ny
    return ((z + far_first(m // ny, nz)) % nz) * ny + (y + far_first(m % ny, ny)) % ny


def row_peer(i, m, nx):
    return ((i // 2 + far_first(m // 2, nx)) % nx) * 2 + (i % 2 + 1 - m % 2) % 2


def expand(x, width):
    e = jnp.where(sub((128, 4 * width)) // 32 == lane((128, 4 * width)) // width, 1.0, 0.0)
    return jnp.dot(x, e, precision=lax.Precision.HIGHEST, preferred_element_type=F32)


def rays_in(x, z, out):
    i, j = sub((128, 512)), lane((128, 512))
    g = j // 128
    e = jnp.where(i == (g // 2) * 64 + (j % 32) * 2 + g % 2, 1.0, 0.0)
    for b in range(4):
        y = jnp.dot(x[:, b * 128:(b + 1) * 128], e, precision=lax.Precision.HIGHEST, preferred_element_type=F32)
        for g in range(4):
            r = (g % 2) * 8 + b * 2 + g // 2
            z[r * 8:r * 8 + 8, :] = y[:, g * 128:(g + 1) * 128]
    grp = lane((1, 128)) // 32
    for h in range(2):
        v = z[pl.ds(h * 4, 16, stride=8), :]
        for s in range(1, 4):
            v = jnp.where(grp == s, z[pl.ds(h * 4 + s, 16, stride=8), :], v)
        out[h] = v


def rays_out(x, z, out):
    grp = lane((1, 128)) // 32
    for h in range(2):
        for s in range(4):
            v = jnp.where(grp == s, x[h], 0.0)
            v = v + pltpu.roll(v, 32, 1)
            z[pl.ds(h * 4 + s, 16, stride=8), :] = v + pltpu.roll(v, 64, 1)
    i, j = sub((128, 128)), lane((128, 128))
    e = jnp.where(i == (j // 64) * 64 + (j % 2) * 32 + (j % 64) // 2, 1.0, 0.0)
    for b in range(4):
        y = None
        for g in range(4):
            r = (g % 2) * 8 + b * 2 + g // 2
            v = z[r * 8:r * 8 + 8, :]
            y = v if g == 0 else jnp.where(grp == g, v, y)
        out[:, b * 128:(b + 1) * 128] = jnp.dot(y, e, precision=lax.Precision.HIGHEST, preferred_element_type=F32)


def pixels_part(x, h, z):
    low = lane((1, 128)) < 64
    for sp in range(2):
        v = x[:, sp * 128:(sp + 1) * 128]
        r = pltpu.roll(v, 64, 1)
        z[pl.ds(h * 4 + 2 * sp, 64, stride=8), :] = jnp.where(low, v, r)
        z[pl.ds(h * 4 + 2 * sp + 1, 64, stride=8), :] = jnp.where(low, r, v)


def pixels_out(z, out):
    low = lane((1, 128)) < 64
    for t in range(32):
        out[:, t * 128:(t + 1) * 128] = jnp.where(low, z[t * 16:t * 16 + 8, :], z[t * 16 + 8:t * 16 + 16, :])


def kernel(nr, nc, ny, rows_s, cols_s, rows_v, cols_v, count, t_hbm, sino, sol_o, res_o, grad_o,
           tv, st, w, wt, ohr, ohc, tb, ta, pb, pa,
           r_all, q0_all, q1_all, rf, g0_all, g1_all, pp, gp, rp, qp, sc,
           g_sh, s_sh, r_sh, q_sh, zr, zs, zg, sems, tsem):
    i, j = lax.axis_index("rows"), lax.axis_index("cols")
    chunks = SL // CHUNK
    for k in range(chunks):
        tile_copy(t_hbm.at[0], tv, tsem, k).start()
    barrier = pltpu.get_barrier_semaphore()

    @pl.loop(0, nc - 1)
    def _(m):
        pl.semaphore_signal(barrier, inc=1, device_id={"cols": col_peer(j, m, ny, nc // ny)}, device_id_type=MESH)

    @pl.loop(0, nr - 1)
    def _(m):
        pl.semaphore_signal(barrier, inc=1, device_id={"rows": row_peer(i, m, nr // 2)}, device_id_type=MESH)

    def to_cols(src, dst, ph, h):
        @pl.loop(0, nc - 1)
        def _(m):
            to = col_peer(j, m, ny, nc // ny)
            pltpu.make_async_remote_copy(src(to), dst.at[j], sems.at[0, ph, h], sems.at[1, ph, h], device_id={"cols": to}, device_id_type=MESH).start()

    def to_rows(src, dst, ph, h):
        @pl.loop(0, nr - 1)
        def _(m):
            to = row_peer(i, m, nr // 2)
            pltpu.make_async_remote_copy(src(to), dst.at[i], sems.at[0, ph, h], sems.at[1, ph, h], device_id={"rows": to}, device_id_type=MESH).start()

    def arrived(buf, n, ph, h):
        wait_bytes(buf, n - 1, sems.at[1, ph, h])

    def left(buf, n, ph, h):
        wait_bytes(buf, n - 1, sems.at[0, ph, h])

    rays_in(sino[...], zr, r_sh)
    for h in range(2):
        r_all[h, j] = r_sh[h].astype(BF)
    build_oh(rows_v, cols_v, count[0, 0], ohr, ohc)
    pl.semaphore_wait(barrier, nc + nr - 2)
    for h in range(2):
        to_cols(lambda to: r_all.at[h, j], r_all.at[h], 0, h)

    for k in range(chunks):
        tile_copy(t_hbm.at[0], tv, tsem, k).wait()

    @pl.loop(0, chunks)
    def _(k):
        build_w(tv, st, w, k)

    def back(h, n, ph):
        table_b(r_all.at[h], tb)
        main(rows_s, tb, w, pb, False, 20)
        parts, buf = pp.at[n, h], gp.at[n, h]
        scatter_b(pb, ohc, parts)
        to_rows(lambda to: parts.at[to], buf, ph, h)
        buf[i] = parts[i]

    def forward(h, n, ph, d_all):
        table_a(d_all, ta)
        main(cols_s, ta, wt, pa, True, 20)
        parts, buf = rp.at[n, h], qp.at[n, h]
        scatter_a(pa, ohr, parts)
        to_cols(lambda to: parts.at[to], buf, ph, h)
        buf[j] = parts[j]

    def total(buf, n, ph, h):
        arrived(buf, n, ph, h)
        return jnp.sum(buf[...].astype(F32), 0)

    def exchange(n, h, vals, ph):
        vals = [jnp.sum(v.reshape(-1, 128), 0, keepdims=True) for v in vals]
        buf = sc.at[n, h]
        buf[i] = jnp.concatenate(vals + [jnp.zeros((8 - len(vals), 128), F32)], 0)
        to_rows(lambda to: buf.at[i], buf, ph, h)

    def exchanged(n, h, ph):
        tot = total(sc.at[n, h], nr, ph, h)
        return expand(tot, 32), expand(tot, 64)

    for h in range(2):
        arrived(r_all.at[h], nc, 0, h)
        back(h, 0, 1)
    build_wt(w, wt, 0, 80)
    for h in range(2):
        g = total(gp.at[0, h], nr, 1, h)
        g_sh[h] = g
        g0_all[h, i] = g.astype(BF)
        to_rows(lambda to: g0_all.at[h, i], g0_all.at[h], 2, h)
    build_wt(w, wt, 80, 160)
    for h in range(2):
        arrived(g0_all.at[h], nr, 2, h)
        forward(h, 0, 3, g0_all.at[h])
    for h in range(2):
        q = total(qp.at[0, h], nc, 3, h)
        q_sh[h] = q
        q0_all[h, j] = q.astype(BF)
        to_cols(lambda to: q0_all.at[h, j], q0_all.at[h], 4, h)
    for h in range(2):
        left(r_all.at[h], nc, 0, h)
        arrived(q0_all.at[h], nc, 4, h)
        r0, q0 = r_all[h].astype(F32), q0_all[h].astype(F32)
        exchange(0, h, [r0 * q0, q0 * q0], 5)
    n32, n64 = [None, None], [None, None]
    for h in range(2):
        n32[h], n64[h] = exchanged(0, h, 5)
        alpha = n32[h][0:1] / (n32[h][1:2] + EPS)
        r1 = r_all[h].astype(F32) - alpha * q0_all[h].astype(F32)
        rf[h] = r1
        r_all[h] = r1.astype(BF)
        back(h, 1, 6)
    for h in range(2):
        alpha, alpha_p = n32[h][0:1] / (n32[h][1:2] + EPS), n64[h][0:1] / (n64[h][1:2] + EPS)
        r_sh[h] = r_sh[h] - alpha * q_sh[h]
        s_sh[h] = alpha_p * g_sh[h]
    for h in range(2):
        g = total(gp.at[1, h], nr, 6, h)
        g1_all[h, i] = g.astype(BF)
        to_rows(lambda to: g1_all.at[h, i], g1_all.at[h], 7, h)
        zg[h] = g
    for h in range(2):
        arrived(g1_all.at[h], nr, 7, h)
        forward(h, 1, 8, g1_all.at[h])
    for h in range(2):
        q = total(qp.at[1, h], nc, 8, h)
        q1_all[h, j] = q.astype(BF)
        to_cols(lambda to: q1_all.at[h, j], q1_all.at[h], 9, h)
        zs[h] = q
    for h in range(2):
        arrived(q1_all.at[h], nc, 9, h)
        q1, q0 = q1_all[h].astype(F32), q0_all[h].astype(F32)
        exchange(1, h, [rf[h] * q1, q1 * q1, q1 * q0], 10)

    def second(n, m):
        beta = m[0:1] / (n[0:1] + EPS)
        delta = m[1:2] + 2.0 * beta * m[2:3] + beta * beta * n[1:2]
        return beta, m[0:1] / (delta + EPS)

    m32, m64 = [None, None], [None, None]
    for h in range(2):
        m32[h], m64[h] = exchanged(1, h, 10)
        beta, alpha = second(n32[h], m32[h])
        r_all[h] = (rf[h] - alpha * (q1_all[h].astype(F32) + beta * q0_all[h].astype(F32))).astype(BF)
        back(h, 2, 11)
    for h in range(2):
        beta, alpha = second(n32[h], m32[h])
        r_sh[h] = r_sh[h] - alpha * (zs[h] + beta * q_sh[h])
        beta, alpha = second(n64[h], m64[h])
        pixels_part(s_sh[h] + alpha * (zg[h] + beta * g_sh[h]), h, zr)
    pixels_out(zr, sol_o)
    rays_out(r_sh, zr, res_o)
    for h in range(2):
        pixels_part(total(gp.at[2, h], nr, 11, h), h, zr)
    pixels_out(zr, grad_o)
    for h in range(2):
        for ph, buf, n in ((1, gp.at[0], nr), (2, g0_all, nr), (3, qp.at[0], nc), (4, q0_all, nc), (5, sc.at[0], nr), (6, gp.at[1], nr),
                           (7, g1_all, nr), (8, qp.at[1], nc), (9, q1_all, nc), (10, sc.at[1], nr), (11, gp.at[2], nr)):
            left(buf.at[h], n, ph, h)


def solution(mesh):
    nr, nc = mesh.shape["rows"], mesh.shape["cols"]
    ny = 4

    def body(sinogram, tiles, tile_rows, tile_cols, tile_counts):
        vm, sm = pl.BlockSpec(memory_space=pltpu.VMEM), pl.BlockSpec(memory_space=pltpu.SMEM)

        def ray(n, t=BF):
            return pltpu.VMEM((*n, nc, 16, 128), t)

        def pix(n):
            return pltpu.VMEM((*n, nr, 64, 256), BF)

        return pl.pallas_call(
            functools.partial(kernel, nr, nc, ny),
            out_shape=(jax.ShapeDtypeStruct((8, 4096), F32), jax.ShapeDtypeStruct((8, 512), F32), jax.ShapeDtypeStruct((8, 4096), F32)),
            in_specs=[sm, sm, vm, vm, sm, pl.BlockSpec(memory_space=pl.ANY), vm],
            out_specs=(vm, vm, vm),
            scratch_shapes=[
                pltpu.VMEM((SL // CHUNK, CHUNK, 4096), BF), pltpu.VMEM((2, CHUNK * PAD, 128), F32),
                pltpu.VMEM((160, 128, 128), BF), pltpu.VMEM((160, 128, 128), BF),
                pltpu.VMEM((256, SL), BF), pltpu.VMEM((512, SL), BF), pltpu.VMEM((256, 8, 128), F32), pltpu.VMEM((512, 8, 128), F32),
                pltpu.VMEM((SL * 8, 128), F32), pltpu.VMEM((160 * PAD, 128), F32),
                ray((2,)), ray((2,)), ray((2,)), ray((2,), F32),
                pix((2,)), pix((2,)), pix((3, 2)), pix((3, 2)), ray((2, 2)), ray((2, 2)), pltpu.VMEM((2, 2, nr, 8, 128), F32),
                pltpu.VMEM((2, 64, 256), F32), pltpu.VMEM((2, 64, 256), F32), pltpu.VMEM((2, 16, 128), F32), pltpu.VMEM((2, 16, 128), F32),
                pltpu.VMEM((512, 128), F32), pltpu.VMEM((2, 16, 128), F32), pltpu.VMEM((2, 64, 256), F32),
                pltpu.SemaphoreType.DMA((2, 12, 2)), pltpu.SemaphoreType.DMA((SL // CHUNK,)),
            ],
            compiler_params=pltpu.CompilerParams(collective_id=0, has_side_effects=True, vmem_limit_bytes=60 * 2**20),
            name="cgls",
        )(tile_rows, tile_cols, tile_rows, tile_cols, tile_counts, tiles, sinogram)

    return jax.shard_map(
        body,
        mesh=mesh,
        in_specs=(
            P(None, ("rows", "cols")),
            P("rows", "cols", None),
            P("rows", "cols"),
            P("rows", "cols"),
            P("rows", "cols"),
        ),
        out_specs=(P(None, ("cols", "rows")), P(None, ("rows", "cols")), P(None, ("cols", "rows"))),
        check_vma=False,
    )
```

time: 1330 us -> 112 us (0.08)
  waiting for transfers between devices: 599 us -> 0 us
  blocking collectives: 381 us -> 0 us
  local copies, waits for them, and re-layouts: 153 us -> 4.46 us
  other arithmetic: 123 us -> 0 us
  Pallas kernels: 0 us -> 106 us
  matrix products: 50.2 us -> 0 us
  between operations: 14.7 us -> 1.29 us
    reduce_scatter x5 -> x0, waiting for transfers between devices: 599 us -> none  [the longest x2 439 us: body(): lax.psum_scatter(tile_loop(tiles, tile_rows, tile_cols, tile_counts, forw...]
    psum x3 -> x0, blocking collectives: 238 us -> none  [the longest x2 158 us: pixel_square(): return lax.psum(partial_value, ('rows', 'cols'))]
    all_gather x5 -> x0, blocking collectives: 143 us -> none  [the longest x3 113 us: ray_group_rounded(): lax.all_gather(values.astype(jnp.bfloat16), 'cols', axis=1, tiled=True)]
    pallas_call x0 -> x1, Pallas kernels: none -> 106 us  [body(): pl.pallas_call(functools.partial(kernel, nr, nc, ny), out_shape=(jax.Shap...]
    scatter-add x20 -> x0, other arithmetic: 98.4 us -> none  [the longest x12 59 us: step(): return total.at[:, column_ids].add(product)]
    reshape x25 -> x0, local copies, waits for them, and re-layouts: 80.1 us -> none  [the longest x20 76.3 us: step(): lax.dynamic_slice_in_dim(plates_all, start, block, 0)]
    dot_general x20 -> x0, matrix products: 50.2 us -> none  [the longest x12 27.6 us: step(): jnp.einsum('str,trc->stc', picked, plates, preferred_element_type=jnp.flo...]
    gather x20 -> x0, local copies, waits for them, and re-layouts: 26.1 us -> none  [the longest x12 20.6 us: step(): picked = jnp.take(table, row_ids, axis=1)]
  transfers between devices with their start and end apart: 5 -> 0, of which waited for: 5 -> 0; matrix products, arithmetic and copies ran while one was open for 0% -> 0% of each run, Pallas kernels for 0% -> 0%
where the time goes in v2:
time: 112 us
  Pallas kernels  106 us (95%)
  local copies, waits for them, and re-layouts  4.46 us (4%)
  between operations  1.29 us (1%)
    pallas_call x1, Pallas kernels, body(): pl.pallas_call(functools.partial(kernel, nr, nc, ny), out_shape=(jax.Shap...  106 us
    unnamed x3, local copies, waits for them, and re-layouts  4.46 us

profile of v2, /device:TPU:1, one launch (start us, length us, event | category | flops | bytes accessed | tf_op | source)
XLA Modules:
  0.0 111.6 jit_solution(12774809729171301428)
XLA Ops:
  1.3 105.8 %cgls.1 = (f32[8,4096]{1,0:T(8,128)}, f32[8,512]{1,0:T(8,128)}, f32[8,4096]{1,0:T(8,128)}) custom-call(s32[1,640]{1,0:T(1,128)} %rows_v.1, s32[1,640]{1,0:T(1,128)} %cols_v.1, s32[1,640]{1,0:T(1,128)} %rows_v.1, s32[1,640]{1,0:T(1,128)} %cols_v.1, s32[1,1]{1,0:T(1,128)S(6)} %copy.11.count, bf16[1,640,4096]{2,1,0:T(8,128)(2,1)} %t_hbm.1, f32[8,512]{1,0:T(8,128)} %sino.1), custom_call_target="tpu_custom_call" | custom-call | tf_op jit(solution)/shard_map/cgls/pallas_call | solution.py:381
  107.1 1.6 %copy.12 = f32[8,4096]{1,0:T(8,128)} copy(f32[8,4096]{1,0:T(8,128)} %get-tuple-element.6) | data formatting | bytes 262144
  108.7 1.3 %copy.13 = f32[8,512]{1,0:T(8,128)} copy(f32[8,512]{1,0:T(8,128)} %get-tuple-element.7) | data formatting | bytes 32768
  110.0 1.6 %copy.14 = f32[8,4096]{1,0:T(8,128)} copy(f32[8,4096]{1,0:T(8,128)} %get-tuple-element.8) | data formatting | bytes 262144

commit v3 on v2

--- a/solution.py
+++ b/solution.py
@@ -102,7 +102,7 @@
             p[pl.ds(pl.multiple_of((o * unroll + u) * pad, 8), 32), :] = out[u]
 
 
-def scatter_b(p, ohc, out):
+def scatter_b(p, ohc, emit):
     low = lane((1, 128)) < 64
     for sp in range(2):
         fs = []
@@ -110,8 +110,7 @@
             m = jnp.where(low, p[pl.ds(s, SL, stride=8), :], p[pl.ds(4 + s, SL, stride=8), :])
             fs.append(m + pltpu.roll(m, 64, 1))
         x = jnp.where(low, fs[0], fs[1]).astype(BF)
-        y = jnp.dot(ohc[...], x, preferred_element_type=F32)
-        out[:, :, sp * 128:(sp + 1) * 128] = y.astype(BF).reshape(8, 64, 128)
+        emit(sp, jnp.dot(ohc[...], x, preferred_element_type=F32))
 
 
 def scatter_a(p, ohr, out):
@@ -136,17 +135,8 @@
     pltpu.make_async_copy(buf.at[pl.ds(0, n)], buf.at[pl.ds(0, n)], sem).wait()
 
 
-def far_first(a, n):
-    return n // 2 + ((a + 1) // 2) * (1 - 2 * (a % 2))
-
-
-def col_peer(j, m, ny, nz):
-    z, y = j // ny, j % ny
-    return ((z + far_first(m // ny, nz)) % nz) * ny + (y + far_first(m % ny, ny)) % ny
-
-
-def row_peer(i, m, nx):
-    return ((i // 2 + far_first(m // 2, nx)) % nx) * 2 + (i % 2 + 1 - m % 2) % 2
+def ring(n):
+    return sorted(range(n), key=lambda d: -min(d, n - d))
 
 
 def expand(x, width):
@@ -206,32 +196,28 @@
 
 def kernel(nr, nc, ny, rows_s, cols_s, rows_v, cols_v, count, t_hbm, sino, sol_o, res_o, grad_o,
            tv, st, w, wt, ohr, ohc, tb, ta, pb, pa,
-           r_all, q0_all, q1_all, rf, g0_all, g1_all, pp, gp, rp, qp, sc,
-           g_sh, s_sh, r_sh, q_sh, zr, zs, zg, sems, tsem):
+           r_all, q0_all, q1_all, sr, sq, s1, g0_all, g1_all, pp, gp, rp, qp, sc,
+           g_sh, r_sh, q_sh, zr, zs, zg, sems, tsem):
     i, j = lax.axis_index("rows"), lax.axis_index("cols")
     chunks = SL // CHUNK
     for k in range(chunks):
         tile_copy(t_hbm.at[0], tv, tsem, k).start()
+    nx, nz = nr // 2, nc // ny
+    x, core, z, y = i // 2, lax.rem(i, 2), j // ny, lax.rem(j, ny)
+    cols = [lax.rem(z + dz, nz) * ny + lax.rem(y + dy, ny) for dz in ring(nz) for dy in ring(ny)][:-1]
+    rows = [lax.rem(x + dx, nx) * 2 + (1 - core if dc else core) for dx in ring(nx) for dc in (1, 0)][:-1]
     barrier = pltpu.get_barrier_semaphore()
-
-    @pl.loop(0, nc - 1)
-    def _(m):
-        pl.semaphore_signal(barrier, inc=1, device_id={"cols": col_peer(j, m, ny, nc // ny)}, device_id_type=MESH)
-
-    @pl.loop(0, nr - 1)
-    def _(m):
-        pl.semaphore_signal(barrier, inc=1, device_id={"rows": row_peer(i, m, nr // 2)}, device_id_type=MESH)
+    for to in cols:
+        pl.semaphore_signal(barrier, inc=1, device_id={"cols": to}, device_id_type=MESH)
+    for to in rows:
+        pl.semaphore_signal(barrier, inc=1, device_id={"rows": to}, device_id_type=MESH)
 
     def to_cols(src, dst, ph, h):
-        @pl.loop(0, nc - 1)
-        def _(m):
-            to = col_peer(j, m, ny, nc // ny)
+        for to in cols:
             pltpu.make_async_remote_copy(src(to), dst.at[j], sems.at[0, ph, h], sems.at[1, ph, h], device_id={"cols": to}, device_id_type=MESH).start()
 
     def to_rows(src, dst, ph, h):
-        @pl.loop(0, nr - 1)
-        def _(m):
-            to = row_peer(i, m, nr // 2)
+        for to in rows:
             pltpu.make_async_remote_copy(src(to), dst.at[i], sems.at[0, ph, h], sems.at[1, ph, h], device_id={"rows": to}, device_id_type=MESH).start()
 
     def arrived(buf, n, ph, h):
@@ -255,17 +241,25 @@
     def _(k):
         build_w(tv, st, w, k)
 
-    def back(h, n, ph):
-        table_b(r_all.at[h], tb)
-        main(rows_s, tb, w, pb, False, 20)
+    def back(h, src):
+        table_b(src.at[h], tb)
+        main(rows_s, tb, w, pb, False, 80)
+
+    def sums_of(to):
+        def emit(sp, y):
+            to[:, sp * 128:(sp + 1) * 128] = y
+
+        scatter_b(pb, ohc, emit)
+
+    def spread(h, n, ph, sums):
         parts, buf = pp.at[n, h], gp.at[n, h]
-        scatter_b(pb, ohc, parts)
+        parts[...] = sums.astype(BF).reshape(nr, 64, 256)
         to_rows(lambda to: parts.at[to], buf, ph, h)
         buf[i] = parts[i]
 
     def forward(h, n, ph, d_all):
         table_a(d_all, ta)
-        main(cols_s, ta, wt, pa, True, 20)
+        main(cols_s, ta, wt, pa, True, 80)
         parts, buf = rp.at[n, h], qp.at[n, h]
         scatter_a(pa, ohr, parts)
         to_cols(lambda to: parts.at[to], buf, ph, h)
@@ -287,39 +281,47 @@
 
     for h in range(2):
         arrived(r_all.at[h], nc, 0, h)
-        back(h, 0, 1)
+        back(h, r_all)
+        sums_of(sr.at[h])
+        spread(h, 0, 1, sr[h])
     build_wt(w, wt, 0, 80)
     for h in range(2):
         g = total(gp.at[0, h], nr, 1, h)
-        g_sh[h] = g
         g0_all[h, i] = g.astype(BF)
         to_rows(lambda to: g0_all.at[h, i], g0_all.at[h], 2, h)
+        g_sh[h] = g
     build_wt(w, wt, 80, 160)
     for h in range(2):
         arrived(g0_all.at[h], nr, 2, h)
         forward(h, 0, 3, g0_all.at[h])
     for h in range(2):
         q = total(qp.at[0, h], nc, 3, h)
-        q_sh[h] = q
         q0_all[h, j] = q.astype(BF)
         to_cols(lambda to: q0_all.at[h, j], q0_all.at[h], 4, h)
-    for h in range(2):
-        left(r_all.at[h], nc, 0, h)
+        q_sh[h] = q
+    n32, n64 = [None, None], [None, None]
+
+    def norms0(h):
         arrived(q0_all.at[h], nc, 4, h)
         r0, q0 = r_all[h].astype(F32), q0_all[h].astype(F32)
         exchange(0, h, [r0 * q0, q0 * q0], 5)
-    n32, n64 = [None, None], [None, None]
-    for h in range(2):
+
+    def step0(h):
         n32[h], n64[h] = exchanged(0, h, 5)
-        alpha = n32[h][0:1] / (n32[h][1:2] + EPS)
-        r1 = r_all[h].astype(F32) - alpha * q0_all[h].astype(F32)
-        rf[h] = r1
-        r_all[h] = r1.astype(BF)
-        back(h, 1, 6)
-    for h in range(2):
-        alpha, alpha_p = n32[h][0:1] / (n32[h][1:2] + EPS), n64[h][0:1] / (n64[h][1:2] + EPS)
-        r_sh[h] = r_sh[h] - alpha * q_sh[h]
-        s_sh[h] = alpha_p * g_sh[h]
+        v = sr[h] - n64[h][0:1] / (n64[h][1:2] + EPS) * sq[h]
+        spread(h, 1, 6, v)
+        sr[h] = v
+
+    norms0(0)
+    back(0, q0_all)
+    sums_of(sq.at[0])
+    norms0(1)
+    step0(0)
+    back(1, q0_all)
+    sums_of(sq.at[1])
+    step0(1)
+    for h in range(2):
+        r_sh[h] = r_sh[h] - n32[h][0:1] / (n32[h][1:2] + EPS) * q_sh[h]
     for h in range(2):
         g = total(gp.at[1, h], nr, 6, h)
         g1_all[h, i] = g.astype(BF)
@@ -333,36 +335,54 @@
         q1_all[h, j] = q.astype(BF)
         to_cols(lambda to: q1_all.at[h, j], q1_all.at[h], 9, h)
         zs[h] = q
-    for h in range(2):
+
+    def norms1(h):
         arrived(q1_all.at[h], nc, 9, h)
-        q1, q0 = q1_all[h].astype(F32), q0_all[h].astype(F32)
-        exchange(1, h, [rf[h] * q1, q1 * q1, q1 * q0], 10)
-
-    def second(n, m):
-        beta = m[0:1] / (n[0:1] + EPS)
+        r0, q0, q1 = r_all[h].astype(F32), q0_all[h].astype(F32), q1_all[h].astype(F32)
+        exchange(1, h, [r0 * q1, q1 * q1, q1 * q0], 10)
+
+    def scalars(n, m):
+        alpha = n[0:1] / (n[1:2] + EPS)
+        gamma = m[0:1] - alpha * m[2:3]
+        beta = gamma / (n[0:1] + EPS)
         delta = m[1:2] + 2.0 * beta * m[2:3] + beta * beta * n[1:2]
-        return beta, m[0:1] / (delta + EPS)
+        return alpha, beta, gamma / (delta + EPS)
 
     m32, m64 = [None, None], [None, None]
-    for h in range(2):
+
+    def step1(h):
         m32[h], m64[h] = exchanged(1, h, 10)
-        beta, alpha = second(n32[h], m32[h])
-        r_all[h] = (rf[h] - alpha * (q1_all[h].astype(F32) + beta * q0_all[h].astype(F32))).astype(BF)
-        back(h, 2, 11)
-    for h in range(2):
-        beta, alpha = second(n32[h], m32[h])
+        _, beta, alpha = scalars(n64[h], m64[h])
+        spread(h, 2, 11, sr[h] - alpha * (s1[...] + beta * sq[h]))
+
+    norms1(0)
+    back(0, q1_all)
+    sums_of(s1)
+    norms1(1)
+    step1(0)
+    back(1, q1_all)
+    sums_of(s1)
+    step1(1)
+    for h in range(2):
+        _, beta, alpha = scalars(n32[h], m32[h])
         r_sh[h] = r_sh[h] - alpha * (zs[h] + beta * q_sh[h])
-        beta, alpha = second(n64[h], m64[h])
-        pixels_part(s_sh[h] + alpha * (zg[h] + beta * g_sh[h]), h, zr)
+        alpha0, beta, alpha = scalars(n64[h], m64[h])
+        pixels_part(alpha0 * g_sh[h] + alpha * (zg[h] + beta * g_sh[h]), h, zr)
     pixels_out(zr, sol_o)
     rays_out(r_sh, zr, res_o)
     for h in range(2):
         pixels_part(total(gp.at[2, h], nr, 11, h), h, zr)
     pixels_out(zr, grad_o)
     for h in range(2):
-        for ph, buf, n in ((1, gp.at[0], nr), (2, g0_all, nr), (3, qp.at[0], nc), (4, q0_all, nc), (5, sc.at[0], nr), (6, gp.at[1], nr),
+        for ph, buf, n in ((0, r_all, nc), (1, gp.at[0], nr), (2, g0_all, nr), (3, qp.at[0], nc), (4, q0_all, nc), (5, sc.at[0], nr), (6, gp.at[1], nr),
                            (7, g1_all, nr), (8, qp.at[1], nc), (9, q1_all, nc), (10, sc.at[1], nr), (11, gp.at[2], nr)):
             left(buf.at[h], n, ph, h)
+
+
+def write(a, b, c, x, y, z):
+    x[...] = a[...]
+    y[...] = b[...]
+    z[...] = c[...]
 
 
 def solution(mesh):
@@ -378,9 +398,10 @@
         def pix(n):
             return pltpu.VMEM((*n, nr, 64, 256), BF)
 
-        return pl.pallas_call(
+        outs = (jax.ShapeDtypeStruct((8, 4096), F32), jax.ShapeDtypeStruct((8, 512), F32), jax.ShapeDtypeStruct((8, 4096), F32))
+        made = pl.pallas_call(
             functools.partial(kernel, nr, nc, ny),
-            out_shape=(jax.ShapeDtypeStruct((8, 4096), F32), jax.ShapeDtypeStruct((8, 512), F32), jax.ShapeDtypeStruct((8, 4096), F32)),
+            out_shape=outs,
             in_specs=[sm, sm, vm, vm, sm, pl.BlockSpec(memory_space=pl.ANY), vm],
             out_specs=(vm, vm, vm),
             scratch_shapes=[
@@ -388,15 +409,22 @@
                 pltpu.VMEM((160, 128, 128), BF), pltpu.VMEM((160, 128, 128), BF),
                 pltpu.VMEM((256, SL), BF), pltpu.VMEM((512, SL), BF), pltpu.VMEM((256, 8, 128), F32), pltpu.VMEM((512, 8, 128), F32),
                 pltpu.VMEM((SL * 8, 128), F32), pltpu.VMEM((160 * PAD, 128), F32),
-                ray((2,)), ray((2,)), ray((2,)), ray((2,), F32),
+                ray((2,)), ray((2,)), ray((2,)), pltpu.VMEM((2, 512, 256), F32), pltpu.VMEM((2, 512, 256), F32), pltpu.VMEM((512, 256), F32),
                 pix((2,)), pix((2,)), pix((3, 2)), pix((3, 2)), ray((2, 2)), ray((2, 2)), pltpu.VMEM((2, 2, nr, 8, 128), F32),
-                pltpu.VMEM((2, 64, 256), F32), pltpu.VMEM((2, 64, 256), F32), pltpu.VMEM((2, 16, 128), F32), pltpu.VMEM((2, 16, 128), F32),
+                pltpu.VMEM((2, 64, 256), F32), pltpu.VMEM((2, 16, 128), F32), pltpu.VMEM((2, 16, 128), F32),
                 pltpu.VMEM((512, 128), F32), pltpu.VMEM((2, 16, 128), F32), pltpu.VMEM((2, 64, 256), F32),
                 pltpu.SemaphoreType.DMA((2, 12, 2)), pltpu.SemaphoreType.DMA((SL // CHUNK,)),
             ],
             compiler_params=pltpu.CompilerParams(collective_id=0, has_side_effects=True, vmem_limit_bytes=60 * 2**20),
             name="cgls",
         )(tile_rows, tile_cols, tile_rows, tile_cols, tile_counts, tiles, sinogram)
+        return pl.pallas_call(
+            write,
+            out_shape=outs,
+            in_specs=[vm] * 3,
+            out_specs=(vm,) * 3,
+            name="write",
+        )(*made)
 
     return jax.shard_map(
         body,

time: 112 us -> 96.4 us (0.86)
  Pallas kernels: 106 us -> 94.9 us
  local copies, waits for them, and re-layouts: 4.46 us -> 0 us
    pallas_call x1 -> x2, Pallas kernels: 106 us -> 94.9 us  [the longest x1 93.2 us: body(): pl.pallas_call(functools.partial(kernel, nr, nc, ny), out_shape=outs, in_...]
    unnamed x3 -> x0, local copies, waits for them, and re-layouts: 4.46 us -> none
where the time goes in v3:
time: 96.4 us; the launch traced here: 96.2 us
  Pallas kernels  94.9 us (98%)
  between operations  1.29 us (1%)
    pallas_call x1, Pallas kernels, body(): pl.pallas_call(functools.partial(kernel, nr, nc, ny), out_shape=outs, in_...  93.2 us

profile of v3, /device:TPU:1, one launch (start us, length us, event | category | flops | bytes accessed | tf_op | source)
XLA Modules:
  0.0 96.2 jit_solution(10226039011588945458)
XLA Ops:
  1.3 93.2 %cgls.1 = (f32[8,4096]{1,0:T(8,128)}, f32[8,512]{1,0:T(8,128)}, f32[8,4096]{1,0:T(8,128)}) custom-call(s32[1,640]{1,0:T(1,128)} %rows_v.1, s32[1,640]{1,0:T(1,128)} %cols_v.1, s32[1,640]{1,0:T(1,128)} %rows_v.1, s32[1,640]{1,0:T(1,128)} %cols_v.1, s32[1,1]{1,0:T(1,128)S(6)} %copy.8.count, bf16[1,640,4096]{2,1,0:T(8,128)(2,1)} %t_hbm.1, f32[8,512]{1,0:T(8,128)} %sino.1), custom_call_target="tpu_custom_call" | custom-call | tf_op jit(solution)/shard_map/cgls/pallas_call | solution.py:402
  94.5 1.7 %write.1 = (f32[8,4096]{1,0:T(8,128)}, f32[8,512]{1,0:T(8,128)}, f32[8,4096]{1,0:T(8,128)}) custom-call(f32[8,4096]{1,0:T(8,128)} %get-tuple-element.6.a, f32[8,512]{1,0:T(8,128)} %get-tuple-element.7.b, f32[8,4096]{1,0:T(8,128)} %get-tuple-element.8.c), custom_call_target="tpu_custom_call" | custom-call | tf_op jit(solution)/shard_map/write/pallas_call | solution.py:421

commit v4 on v3

--- a/solution.py
+++ b/solution.py
@@ -86,20 +86,27 @@
     half = (lane((8, 128)) // 64) == (sub((8, 128)) // 4)
 
     pad = PAD if forward else 32
-
-    @pl.loop(0, SL // 4 // unroll)
+    zero = jnp.zeros((32, 128), BF)
+
+    @pl.loop(0, SL // 8 // unroll)
     def _(o):
         lhs, out = [], []
         for u in range(unroll):
             ls = []
-            for k in range(4):
-                t = idx[0, (o * unroll + u) * 4 + k]
-                ls.append(jnp.where(half if forward else grp == k, tab[t], 0.0))
-            lhs.append(jnp.concatenate(ls, 0).astype(BF))
+            for g in range(2):
+                rs = []
+                for k in range(4):
+                    t = idx[0, (o * unroll + u) * 8 + g * 4 + k]
+                    rs.append(jnp.where(half if forward else grp == k, tab[t], 0.0))
+                v = jnp.concatenate(rs, 0).astype(BF)
+                ls.append(jnp.concatenate([zero, v] if g else [v, zero], 1))
+            lhs.append(jnp.concatenate(ls, 0))
         for u in range(unroll):
-            out.append(jnp.dot(lhs[u], w[o * unroll + u], preferred_element_type=F32))
+            rhs = w[pl.ds((o * unroll + u) * 2, 2)].reshape(256, 128)
+            out.append(jnp.dot(lhs[u], rhs, preferred_element_type=F32))
         for u in range(unroll):
-            p[pl.ds(pl.multiple_of((o * unroll + u) * pad, 8), 32), :] = out[u]
+            for g in range(2):
+                p[pl.ds(pl.multiple_of(((o * unroll + u) * 2 + g) * pad, 8), 32), :] = out[u][g * 32:g * 32 + 32]
 
 
 def scatter_b(p, ohc, emit):
@@ -243,7 +250,7 @@
 
     def back(h, src):
         table_b(src.at[h], tb)
-        main(rows_s, tb, w, pb, False, 80)
+        main(rows_s, tb, w, pb, False, 20)
 
     def sums_of(to):
         def emit(sp, y):
@@ -259,7 +266,7 @@
 
     def forward(h, n, ph, d_all):
         table_a(d_all, ta)
-        main(cols_s, ta, wt, pa, True, 80)
+        main(cols_s, ta, wt, pa, True, 20)
         parts, buf = rp.at[n, h], qp.at[n, h]
         scatter_a(pa, ohr, parts)
         to_cols(lambda to: parts.at[to], buf, ph, h)
@@ -279,7 +286,8 @@
         tot = total(sc.at[n, h], nr, ph, h)
         return expand(tot, 32), expand(tot, 64)
 
-    for h in range(2):
+    @pl.loop(0, 2)
+    def _(h):
         arrived(r_all.at[h], nc, 0, h)
         back(h, r_all)
         sums_of(sr.at[h])
@@ -291,7 +299,8 @@
         to_rows(lambda to: g0_all.at[h, i], g0_all.at[h], 2, h)
         g_sh[h] = g
     build_wt(w, wt, 80, 160)
-    for h in range(2):
+    @pl.loop(0, 2)
+    def _(h):
         arrived(g0_all.at[h], nr, 2, h)
         forward(h, 0, 3, g0_all.at[h])
     for h in range(2):
@@ -327,7 +336,8 @@
         g1_all[h, i] = g.astype(BF)
         to_rows(lambda to: g1_all.at[h, i], g1_all.at[h], 7, h)
         zg[h] = g
-    for h in range(2):
+    @pl.loop(0, 2)
+    def _(h):
         arrived(g1_all.at[h], nr, 7, h)
         forward(h, 1, 8, g1_all.at[h])
     for h in range(2):

time: 96.4 us -> 95.1 us (0.987)
  Pallas kernels: 94.9 us -> 93.2 us
    pallas_call x1, Pallas kernels: 93.2 us -> 91.5 us  [body(): pl.pallas_call(functools.partial(kernel, nr, nc, ny), out_shape=outs, in_...]
where the time goes in v4:
time: 95.1 us; the launch traced here: 94.5 us
  Pallas kernels  93.2 us (98%)
  between operations  1.29 us (1%)
    pallas_call x1, Pallas kernels, body(): pl.pallas_call(functools.partial(kernel, nr, nc, ny), out_shape=outs, in_...  91.5 us

profile of v4, /device:TPU:1, one launch (start us, length us, event | category | flops | bytes accessed | tf_op | source)
XLA Modules:
  0.0 94.5 jit_solution(1103841506378404615)
XLA Ops:
  1.3 91.5 %cgls.1 = (f32[8,4096]{1,0:T(8,128)}, f32[8,512]{1,0:T(8,128)}, f32[8,4096]{1,0:T(8,128)}) custom-call(s32[1,640]{1,0:T(1,128)} %rows_v.1, s32[1,640]{1,0:T(1,128)} %cols_v.1, s32[1,640]{1,0:T(1,128)} %rows_v.1, s32[1,640]{1,0:T(1,128)} %cols_v.1, s32[1,1]{1,0:T(1,128)S(6)} %copy.8.count, bf16[1,640,4096]{2,1,0:T(8,128)(2,1)} %t_hbm.1, f32[8,512]{1,0:T(8,128)} %sino.1), custom_call_target="tpu_custom_call" | custom-call | tf_op jit(solution)/shard_map/cgls/pallas_call | solution.py:412
  92.8 1.7 %write.1 = (f32[8,4096]{1,0:T(8,128)}, f32[8,512]{1,0:T(8,128)}, f32[8,4096]{1,0:T(8,128)}) custom-call(f32[8,4096]{1,0:T(8,128)} %get-tuple-element.6.a, f32[8,512]{1,0:T(8,128)} %get-tuple-element.7.b, f32[8,4096]{1,0:T(8,128)} %get-tuple-element.8.c), custom_call_target="tpu_custom_call" | custom-call | tf_op jit(solution)/shard_map/write/pallas_call | solution.py:431

commit v5 on v4

--- a/solution.py
+++ b/solution.py
@@ -258,11 +258,16 @@
 
         scatter_b(pb, ohc, emit)
 
+    def spread_pair(h, n, ph, sp, y):
+        at = pl.ds(sp * 128, 128)
+        parts, buf = pp.at[n, h], gp.at[n, h]
+        parts[:, :, at] = y.astype(BF).reshape(nr, 64, 128)
+        to_rows(lambda to: parts.at[to, :, at], buf.at[:, :, at], ph, h)
+
     def spread(h, n, ph, sums):
-        parts, buf = pp.at[n, h], gp.at[n, h]
-        parts[...] = sums.astype(BF).reshape(nr, 64, 256)
-        to_rows(lambda to: parts.at[to], buf, ph, h)
-        buf[i] = parts[i]
+        for sp in range(2):
+            spread_pair(h, n, ph, sp, sums[:, sp * 128:(sp + 1) * 128])
+        gp[n, h, i] = pp[n, h, i]
 
     def forward(h, n, ph, d_all):
         table_a(d_all, ta)
@@ -290,8 +295,13 @@
     def _(h):
         arrived(r_all.at[h], nc, 0, h)
         back(h, r_all)
-        sums_of(sr.at[h])
-        spread(h, 0, 1, sr[h])
+
+        def emit(sp, y):
+            sr[h, :, sp * 128:(sp + 1) * 128] = y
+            spread_pair(h, 0, 1, sp, y)
+
+        scatter_b(pb, ohc, emit)
+        gp[0, h, i] = pp[0, h, i]
     build_wt(w, wt, 0, 80)
     for h in range(2):
         g = total(gp.at[0, h], nr, 1, h)

time: 95.1 us -> 96.3 us (1.013)
  Pallas kernels: 93.2 us -> 94.8 us
    pallas_call x1, Pallas kernels: 91.5 us -> 93.1 us  [body(): pl.pallas_call(functools.partial(kernel, nr, nc, ny), out_shape=outs, in_...]
where the time goes in v5:
time: 96.3 us; the launch traced here: 96.1 us
  Pallas kernels  94.8 us (98%)
  between operations  1.29 us (1%)
    pallas_call x1, Pallas kernels, body(): pl.pallas_call(functools.partial(kernel, nr, nc, ny), out_shape=outs, in_...  93.1 us

profile of v5, /device:TPU:1, one launch (start us, length us, event | category | flops | bytes accessed | tf_op | source)
XLA Modules:
  0.0 96.1 jit_solution(13242812223477935441)
XLA Ops:
  1.3 93.1 %cgls.1 = (f32[8,4096]{1,0:T(8,128)}, f32[8,512]{1,0:T(8,128)}, f32[8,4096]{1,0:T(8,128)}) custom-call(s32[1,640]{1,0:T(1,128)} %rows_v.1, s32[1,640]{1,0:T(1,128)} %cols_v.1, s32[1,640]{1,0:T(1,128)} %rows_v.1, s32[1,640]{1,0:T(1,128)} %cols_v.1, s32[1,1]{1,0:T(1,128)S(6)} %copy.8.count, bf16[1,640,4096]{2,1,0:T(8,128)(2,1)} %t_hbm.1, f32[8,512]{1,0:T(8,128)} %sino.1), custom_call_target="tpu_custom_call" | custom-call | tf_op jit(solution)/shard_map/cgls/pallas_call | solution.py:422
  94.4 1.7 %write.1 = (f32[8,4096]{1,0:T(8,128)}, f32[8,512]{1,0:T(8,128)}, f32[8,4096]{1,0:T(8,128)}) custom-call(f32[8,4096]{1,0:T(8,128)} %get-tuple-element.6.a, f32[8,512]{1,0:T(8,128)} %get-tuple-element.7.b, f32[8,4096]{1,0:T(8,128)} %get-tuple-element.8.c), custom_call_target="tpu_custom_call" | custom-call | tf_op jit(solution)/shard_map/write/pallas_call | solution.py:441
